TPU v7x, 128 devices: a whole 4x4x4 slice. The times are simulated.
128 devices in a mesh: row: 8 (over z, core), col: 16 (over y, x).
Axes of the slice: x: 4, y: 4, z: 4, core: 2. Of those that a mesh axis runs over, the one named last changes fastest.
Arguments:
- working: float32 [8, 8, 256, 4, 16, 256], P(None, 'row', None, None, 'col'), may hold values from -6 to 6
- factor_panel: float32 [2, 8, 8, 256, 256], P(None, None, 'row'), may hold values from -0.12 to 2, as said below
Outputs:
- gram_part: float32 [8, 8, 256, 4, 16, 256], P(None, 'row', None, None, 'col')
- finished_columns: float32 [4, 8, 256, 16, 8, 128], P(None, None, None, 'col', 'row')
Inputs may be any that keep to these rules, and one draw needn't show every extreme that they name: factor_panel holds a lower-triangular factor: entries above the factor's diagonal are zero and its diagonal entries lie between 1 and 2.
All inputs are finite; a program needn't handle non-finite values.
Results may differ from a plain program's by a relative error of at most 0.0001.
Values sent between devices are 32-bit elements; how exact they have to be, the bound alone decides.
A program may use at most 192 MiB of HBM per device.

v0:
```python
import jax
import jax.numpy as jnp
from jax import lax
from jax.sharding import PartitionSpec as P

BLK = 256
K = 30
STEPS = 2


def picked(value, axis, root):
    return lax.dynamic_index_in_dim(lax.all_gather(value, axis), root, 0, keepdims=False)


def per_device(working, factor_panel):
    row_count = lax.axis_size("row")
    col_count = lax.axis_size("col")
    row_index = lax.axis_index("row")
    blocks_rows = working.shape[0]
    width = working.shape[2]
    blocks_cols = working.shape[3]
    matrix_rows = working.reshape(blocks_rows, width, blocks_cols * width)
    global_block = jnp.arange(blocks_rows) * row_count + row_index

    def solve_row(slab, step_index):
        target = K + step_index
        owner = target % row_count
        diagonal = jnp.tril(factor_panel[step_index, target // row_count, 0])
        diagonal = jnp.where(row_index == owner, diagonal, jnp.eye(width, dtype=jnp.float32))
        solved = lax.linalg.triangular_solve(diagonal, slab, left_side=True, lower=True)
        return picked(solved, "row", owner)

    def eliminate(rows_part, blocks_part, column_part, solved, step_index):
        target = K + step_index
        updated = rows_part - jnp.einsum(
            "rab,bc->rac", column_part, solved, precision=lax.Precision.HIGHEST
        )
        below = (blocks_part > target)[:, None, None]
        here = (blocks_part == target)[:, None, None]
        return jnp.where(below, updated, jnp.where(here, solved[None], rows_part))

    solved_list = []
    solved = solve_row(matrix_rows[K // row_count], 0)
    for step_index in range(STEPS):
        solved_list.append(solved)
        if step_index + 1 < STEPS:
            slot = (K + step_index + 1) // row_count
            next_slab = eliminate(
                matrix_rows[slot : slot + 1],
                global_block[slot : slot + 1],
                factor_panel[step_index, slot : slot + 1, 0],
                solved,
                step_index,
            )
            following = solve_row(next_slab[0], step_index + 1)
        matrix_rows = eliminate(
            matrix_rows, global_block, factor_panel[step_index, :, 0], solved, step_index
        )
        if step_index + 1 < STEPS:
            solved = following
    stacked = jnp.concatenate(solved_list, 0)
    depth = stacked.shape[0]
    owners_count = col_count // row_count
    gathered = lax.all_gather(
        stacked.reshape(depth, blocks_cols, 1, width), "col", axis=2, tiled=True
    )
    gathered = gathered.reshape(depth, blocks_cols, owners_count, row_count, width)
    chosen = lax.dynamic_index_in_dim(gathered, row_index, 3, keepdims=False)
    row_panels = chosen.reshape(depth, blocks_rows * width)
    gram = lax.dot_general(
        row_panels, stacked, (((0,), (0,)), ((), ())), precision=lax.Precision.HIGHEST
    )
    gram = (gram * (1.0 / (STEPS * BLK))).reshape(blocks_rows, 1, width, blocks_cols, 1, width)
    finished_count = (K + STEPS) // row_count
    finished = matrix_rows[:finished_count].reshape(finished_count, 1, width, 1, row_count, -1)
    moved = lax.all_to_all(finished, "row", split_axis=4, concat_axis=1, tiled=True)
    return (gram, moved)


def solution(mesh):
    placed = (P(None, "row", None, None, "col", None), P(None, None, "row", None, None))
    return jax.shard_map(
        per_device,
        mesh=mesh,
        in_specs=placed,
        out_specs=(
            P(None, "row", None, None, "col", None),
            P(None, None, None, "col", "row", None),
        ),
        check_vma=False,
    )
```

profile of v0, /device:TPU:1, one launch (start us, length us, event | category | flops | bytes accessed | tf_op | source)
XLA Modules:
  0.0 434.1 jit_solution(2634957382837194387)
XLA Ops:
  7.2 0.0 all-gather.8.cloned.1.call-start
  7.2 1.1 fusion.16
  8.3 0.1 broadcast.89
  8.4 3.8 while.4
  8.4 0.6 fusion.36
  9.0 1.3 bitcast_dynamic-update-slice_fusion.4
  10.3 0.6 fusion.36
  10.9 1.3 bitcast_dynamic-update-slice_fusion.4
  12.2 19.7 %custom-call.4 = f32[2,128,128]{1,2,0:T(8,128)S(1)} custom-call(f32[2,128,128]{2,1,0:T(8,128)S(1)} %get-tuple-element.17), custom_call_target="InvertDiagBlocksLowerTriangular" | custom-call | tf_op jit(solution)/shard_map/triangular_solve/custom-call.1 | solution.py:30
  31.9 4.2 slice_reduce_fusion
  36.0 0.2 copy.57
  36.3 0.6 fusion.13
  36.9 0.6 convolution_subtract_fusion.1
  37.5 0.6 fusion.22
  38.1 1.0 pad_maximum_fusion.1
  39.2 0.0 all-gather.8.cloned.1.call-update
  39.2 0.6 all-gather.10.cloned.1.call-start
  39.8 0.6 slice.46
  41.7 0.5 slice.47
  42.2 4.1 while.5
  42.2 0.7 fusion.37
  42.9 1.3 bitcast_dynamic-update-slice_fusion.5
  44.3 0.7 fusion.37
  44.9 1.3 bitcast_dynamic-update-slice_fusion.5
  46.3 19.7 %custom-call.5 = f32[2,128,128]{1,2,0:T(8,128)S(1)} custom-call(f32[2,128,128]{2,1,0:T(8,128)S(1)} %get-tuple-element.18), custom_call_target="InvertDiagBlocksLowerTriangular" | custom-call | tf_op jit(solution)/shard_map/triangular_solve/custom-call.1 | solution.py:30
  66.0 27.0 %all-gather.8.cloned.1.call-done = f32[2048,1024]{1,0:T(8,128)} async-done(((f32[256,1024]{1,0:T(8,128)}), f32[2048,1024]{1,0:T(8,128)}) %all-gather.8.cloned.1.call-update) | async-done | bytes 8388624 | tf_op jit(solution)/shard_map/all_gather | solution.py:12
  93.0 2.9 fusion.8
  95.8 0.6 fusion.11
  96.5 0.6 convolution_subtract_fusion
  97.1 0.6 fusion.20
  97.7 1.0 pad_maximum_fusion.2
  98.7 0.0 all-gather.10.cloned.1.call-update
  98.8 0.2 all-gather.6.cloned.1.call-start
  99.0 1.3 slice.86
  100.3 0.5 concatenate.13
  100.8 1.2 copy.38
  101.9 47.1 %all-gather.10.cloned.1.call-done = f32[2048,1024]{1,0:T(8,128)} async-done(((f32[256,1024]{1,0:T(8,128)}), f32[2048,1024]{1,0:T(8,128)}) %all-gather.10.cloned.1.call-update) | async-done | bytes 8388624 | tf_op jit(solution)/shard_map/all_gather | solution.py:12
  149.1 1.3 slice.92
  150.4 0.5 concatenate.14
  150.9 0.2 copy.39
  151.1 2.8 pad_maximum_fusion
  153.9 0.0 all-gather.6.cloned.1.call-update
  153.9 20.9 %copy.42 = f32[8,1,256,4,1,256]{2,5,3,0,4,1:T(8,128)} copy(f32[8,1,256,4,1,256]{5,4,3,2,1,0:T(1,128)} %param.4) | data formatting | bytes 16777216 | tf_op args[0]
  174.8 0.3 copy.45
  175.1 17.2 %convolution_bitcast_fusion.1 = f32[8,256,1024]{1,2,0:T(8,128)} fusion(f32[2,8,1,256,256]{4,3,1,2,0:T(8,128)} %bitcast.110, f32[2048,1024]{1,0:T(8,128)} %all-gather.8.cloned.1.call-done), kind=kOutput, calls=%fused_computation.11 | convolution fusion | flops 6442450944 | bytes 11534336 | tf_op jit(solution)/shard_map/rab,bc->rac/dot_general | solution.py:35
  192.3 1.3 copy.48
  193.6 0.0 copy-start
  193.6 0.0 copy-start.1
  193.6 16.5 %convolution_bitcast_fusion = f32[8,256,1024]{1,2,0:T(8,128)S(1)} fusion(f32[2,8,1,256,256]{4,3,1,2,0:T(8,128)} %bitcast.111, f32[2048,1024]{1,0:T(8,128)} %all-gather.10.cloned.1.call-done), kind=kOutput, calls=%fused_computation.10 | convolution fusion | flops 6442450944 | bytes 11534336 | tf_op jit(solution)/shard_map/rab,bc->rac/dot_general | solution.py:35
  210.2 0.0 copy-done
  210.2 0.0 copy-done.1
  210.2 4.9 %fusion = f32[4,256,1024]{1,2,0:T(8,128)} fusion(f32[8,256,1024]{1,2,0:T(8,128)S(1)} %convolution_bitcast_fusion, f32[8,256,1024]{1,2,0:T(8,128)S(1)} %copy-done, f32[8,256,1024]{1,2,0:T(8,128)} %bitcast.108, f32[256,1024]{0,1:T(8,128)S(1)} %copy-done.1, f32[256,1024]{0,1:T(8,128)S(1)} %copy.45, pred[4]{0:T(512)(128)(4,1)S(1)} %bitcast.117, ...), kind=kLoop, calls=%fused_computation.7 | loop fusion | flops 6291456 | bytes 18874384 | tf_op jit(solution)/shard_map/jit(_where)/select_n | solution.py:40
  215.1 5.7 %copy.49 = f32[4,1,256,1,8,128]{5,2,0,3,1,4:T(8,128)} copy(f32[4,1,256,1,8,128]{2,5,4,0,3,1:T(8,128)} %bitcast.109) | data formatting | bytes 8388608 | tf_op jit(solution)/shard_map/reshape | solution.py:75
  220.9 4.7 %all-to-all-start = ((f32[4,1,256,1,8,128]{5,2,0,3,1,4:T(8,128)}), f32[4,1,256,1,8,128]{5,2,0,3,1,4:T(8,128)}, u32[]{:S(2)}, u32[]{:S(2)}) async-start(f32[4,1,256,1,8,128]{5,2,0,3,1,4:T(8,128)} %copy.49), calls=%async_computation | async-start | bytes 8388608 | tf_op jit(solution)/shard_map/all_to_all | solution.py:76
  225.5 48.9 %all-to-all-done = f32[4,1,256,1,8,128]{5,2,0,3,1,4:T(8,128)} async-done(((f32[4,1,256,1,8,128]{5,2,0,3,1,4:T(8,128)}), f32[4,1,256,1,8,128]{5,2,0,3,1,4:T(8,128)}, u32[]{:S(2)}, u32[]{:S(2)}) %all-to-all-start) | async-done | bytes 4194336 | tf_op jit(solution)/shard_map/all_to_all | solution.py:76
  274.5 11.4 %copy.51 = f32[4,8,256,1,1,128]{5,4,3,2,1,0:T(1,128)} copy(f32[4,8,256,1,1,128]{5,2,0,1,4,3:T(8,128)} %bitcast.26) | data formatting | bytes 8388608
  285.8 64.7 %all-gather.6.cloned.1.call-done = f32[512,4,16,256]{3,0,1,2:T(8,128)} async-done(((f32[512,4,1,256]{3,0,1,2:T(8,128)}), f32[512,4,16,256]{3,0,1,2:T(8,128)}) %all-gather.6.cloned.1.call-update) | async-done | bytes 33554448 | tf_op jit(solution)/shard_map/all_gather | solution.py:64
  350.6 28.3 %copy.59 = f32[512,4,16,256]{3,2,1,0:T(8,128)S(1)} copy(f32[512,4,16,256]{3,0,1,2:T(8,128)} %all-gather.6.cloned.1.call-done) | data formatting | bytes 67108864 | tf_op jit(solution)/shard_map/all_gather | solution.py:64
  378.8 6.6 %constant_dynamic-slice_fusion.2 = f32[512,4,2,1,256]{4,3,2,1,0:T(1,128)} fusion(f32[512,4,2,8,256]{4,3,2,1,0:T(8,128)S(1)} %bitcast.106, s32[]{:T(128)S(6)} %select_n.57), kind=kLoop, calls=%fused_computation.59 | loop fusion | bytes 8388612 | tf_op jit(solution)/shard_map/jit(dynamic_index_in_dim)/dynamic_slice | solution.py:68
  385.5 10.9 %copy.41 = f32[512,4,2,1,256]{0,4,2,1,3:T(8,128)} copy(f32[512,4,2,1,256]{4,3,2,1,0:T(1,128)} %constant_dynamic-slice_fusion.2) | data formatting | bytes 8388608 | tf_op jit(solution)/shard_map/jit(dynamic_index_in_dim)/dynamic_slice | solution.py:68
  396.4 17.5 %convolution_multiply_fusion = f32[2048,1024]{1,0:T(8,128)} fusion(f32[512,2048]{0,1:T(8,128)} %bitcast.107, f32[256,1024]{1,0:T(8,128)S(1)} %slice.92, f32[256,1024]{1,0:T(8,128)S(1)} %slice.86), kind=kOutput, calls=%fused_computation.5 | convolution fusion | flops 12887523328 | bytes 14680064 | tf_op jit(solution)/shard_map/dot_general | solution.py:70
  413.9 13.5 %reshape.102 = f32[8,1,256,4,1,256]{5,4,3,2,1,0:T(1,128)} reshape(f32[2048,1024]{1,0:T(8,128)} %convolution_multiply_fusion) | data formatting | bytes 16777216 | tf_op jit(solution)/shard_map/reshape | solution.py:73
  (10 shorter events, 0.1 us)
Async XLA Ops:
  7.2 85.8 %all-gather.8.cloned.1.call-start = ((), (), s32[]{:S(2)}) async-start(), calls=%async_computation.2 | async-start | bytes 9437184 | tf_op jit(solution)/shard_map/all_gather | solution.py:12
  39.2 109.9 %all-gather.10.cloned.1.call-start = ((), (), s32[]{:S(2)}) async-start(), calls=%async_computation.3 | async-start | bytes 9437184 | tf_op jit(solution)/shard_map/all_gather | solution.py:12
  98.8 251.8 %all-gather.6.cloned.1.call-start = ((), (), s32[]{:S(2)}) async-start(), calls=%async_computation.1 | async-start | bytes 35651584 | tf_op jit(solution)/shard_map/all_gather | solution.py:64
  193.6 16.6 %copy-start = (f32[8,256,1024]{1,2,0:T(8,128)S(1)}, f32[8,256,1024]{1,2,0:T(8,128)}, u32[]{:S(2)}) copy-start(f32[8,256,1024]{1,2,0:T(8,128)} %convolution_bitcast_fusion.1) | copy-start | bytes 25165828
  193.6 16.6 %copy-start.1 = (f32[256,1024]{0,1:T(8,128)S(1)}, f32[256,1024]{0,1:T(8,128)}, u32[]{:S(2)}) copy-start(f32[256,1024]{0,1:T(8,128)} %copy.48) | copy-start | bytes 3145732
  220.9 53.6 %all-to-all-start = ((f32[4,1,256,1,8,128]{5,2,0,3,1,4:T(8,128)}), f32[4,1,256,1,8,128]{5,2,0,3,1,4:T(8,128)}, u32[]{:S(2)}, u32[]{:S(2)}) async-start(f32[4,1,256,1,8,128]{5,2,0,3,1,4:T(8,128)} %copy.49), calls=%async_computation | async-start | bytes 8388608 | tf_op jit(solution)/shard_map/all_to_all | solution.py:76
Sparse Core Ops, SparseCore 0:
  39.3 53.6 all-gather.7
  98.9 50.1 all-gather.9
  154.0 196.5 all-gather.5
where the time goes:
time: 441 us; the launch traced here: 434 us
  waiting for transfers between devices  188 us (43%)
  local copies, waits for them, and re-layouts  117 us (27%)
  matrix products  57.8 us (13%)
  other arithmetic  50.2 us (11%)
  between operations  15.5 us (4%)
  starting transfers between devices  5.49 us (1%)
    all_gather x2, waiting for transfers between devices, picked(): lax.all_gather(value, axis)  74.1 us
    all_gather x1, waiting for transfers between devices, per_device(): lax.all_gather(stacked.reshape(depth, blocks_cols, 1, width), 'col', axis...  64.7 us
    all_to_all x1, waiting for transfers between devices, per_device(): lax.all_to_all(finished, 'row', split_axis=4, concat_axis=1, tiled=True)  48.9 us
    another operation x6, other arithmetic, solve_row(): lax.linalg.triangular_solve(diagonal, slab, left_side=True, lower=True)  42.5 us
    dot_general x3, matrix products, eliminate(): jnp.einsum('rab,bc->rac', column_part, solved, precision=lax.Precision.HI...  36.6 us
    unnamed x7, local copies, waits for them, and re-layouts  32.5 us
    all_gather x1, local copies, waits for them, and re-layouts, per_device(): lax.all_gather(stacked.reshape(depth, blocks_cols, 1, width), 'col', axis...  28.3 us
    dynamic_slice x2, local copies, waits for them, and re-layouts, per_device(): chosen = lax.dynamic_index_in_dim(gathered, row_index, 3, keepdims=False)  17.6 us
  transfers between devices with their start and end apart: 4, of which 4 were waited for; matrix products, arithmetic and copies ran while one was open for 24% of the time, Pallas kernels for 0%

commit v1 on v0

--- a/solution.py
+++ b/solution.py
@@ -73,7 +73,10 @@
     gram = (gram * (1.0 / (STEPS * BLK))).reshape(blocks_rows, 1, width, blocks_cols, 1, width)
     finished_count = (K + STEPS) // row_count
     finished = matrix_rows[:finished_count].reshape(finished_count, 1, width, 1, row_count, -1)
-    moved = lax.all_to_all(finished, "row", split_axis=4, concat_axis=1, tiled=True)
+    moved = jnp.concatenate(
+        lax.all_to_all(jnp.stack(jnp.split(finished, lax.axis_size("row"), axis=4)), "row", 0, 0),
+        axis=1,
+    )
     return (gram, moved)
 
 

time: 441 us -> 442 us (level)
  local copies, waits for them, and re-layouts: 117 us -> 139 us
  waiting for transfers between devices: 188 us -> 168 us
    unnamed x7 -> x30, local copies, waits for them, and re-layouts: 32.5 us -> 57 us
    all_gather x1, waiting for transfers between devices: 64.7 us -> 44.9 us  [per_device(): lax.all_gather(stacked.reshape(depth, blocks_cols, 1, width), 'col', axis...]
    reshape x1 -> x0, local copies, waits for them, and re-layouts: 5.71 us -> none  [per_device(): matrix_rows[:finished_count]]
  transfers between devices with their start and end apart: 4 -> 4, of which waited for: 4 -> 4; matrix products, arithmetic and copies ran while one was open for 24% -> 29% of each run, Pallas kernels for 0% -> 0%
where the time goes in v1:
time: 442 us; the launch traced here: 434 us
  waiting for transfers between devices  168 us (38%)
  local copies, waits for them, and re-layouts  139 us (31%)
  matrix products  57.9 us (13%)
  other arithmetic  48.1 us (11%)
  between operations  15.5 us (4%)
  starting transfers between devices  5.59 us (1%)
    all_gather x2, waiting for transfers between devices, picked(): lax.all_gather(value, axis)  74.1 us
    unnamed x30, local copies, waits for them, and re-layouts  57 us
    all_to_all x1, waiting for transfers between devices, per_device(): lax.all_to_all(jnp.stack(jnp.split(finished, lax.axis_size('row'), axis=4...  48.9 us
    all_gather x1, waiting for transfers between devices, per_device(): lax.all_gather(stacked.reshape(depth, blocks_cols, 1, width), 'col', axis...  44.9 us
    another operation x6, other arithmetic, solve_row(): lax.linalg.triangular_solve(diagonal, slab, left_side=True, lower=True)  42.5 us
    dot_general x3, matrix products, eliminate(): jnp.einsum('rab,bc->rac', column_part, solved, precision=lax.Precision.HI...  36.7 us
    all_gather x1, local copies, waits for them, and re-layouts, per_device(): lax.all_gather(stacked.reshape(depth, blocks_cols, 1, width), 'col', axis...  28.3 us
    dynamic_slice x2, local copies, waits for them, and re-layouts, per_device(): chosen = lax.dynamic_index_in_dim(gathered, row_index, 3, keepdims=False)  17.6 us
  transfers between devices with their start and end apart: 4, of which 4 were waited for; matrix products, arithmetic and copies ran while one was open for 29% of the time, Pallas kernels for 0%

profile of v1, /device:TPU:1, one launch (start us, length us, event | category | flops | bytes accessed | tf_op | source)
XLA Modules:
  0.0 434.4 jit_solution(11706157244480211859)
XLA Ops:
  7.2 1.1 fusion.16
  8.4 4.0 while.4
  8.4 0.6 fusion.37
  9.0 1.4 bitcast_dynamic-update-slice_fusion.12
  10.4 0.6 fusion.37
  11.0 1.4 bitcast_dynamic-update-slice_fusion.12
  12.4 19.7 %custom-call.4 = f32[2,128,128]{1,2,0:T(8,128)S(1)} custom-call(f32[2,128,128]{2,1,0:T(8,128)S(1)} %get-tuple-element.17), custom_call_target="InvertDiagBlocksLowerTriangular" | custom-call | tf_op jit(solution)/shard_map/triangular_solve/custom-call.1 | solution.py:30
  32.1 4.2 slice_reduce_fusion
  36.4 0.6 fusion.13
  37.1 0.6 convolution_subtract_fusion.1
  37.6 0.6 fusion.22
  38.3 1.0 pad_maximum_fusion.1
  39.4 0.6 all-gather.10.cloned.1.call-start
  39.9 0.6 slice.46
  41.8 0.5 slice.47
  42.4 4.1 while.5
  42.4 0.6 fusion.38
  43.0 1.4 bitcast_dynamic-update-slice_fusion.13
  44.4 0.6 fusion.38
  45.0 1.4 bitcast_dynamic-update-slice_fusion.13
  46.5 19.7 %custom-call.5 = f32[2,128,128]{1,2,0:T(8,128)S(1)} custom-call(f32[2,128,128]{2,1,0:T(8,128)S(1)} %get-tuple-element.18), custom_call_target="InvertDiagBlocksLowerTriangular" | custom-call | tf_op jit(solution)/shard_map/triangular_solve/custom-call.1 | solution.py:30
  66.1 27.0 %all-gather.8.cloned.1.call-done = f32[2048,1024]{1,0:T(8,128)} async-done(((f32[256,1024]{1,0:T(8,128)}), f32[2048,1024]{1,0:T(8,128)}) %all-gather.8.cloned.1.call-update) | async-done | bytes 8388624 | tf_op jit(solution)/shard_map/all_gather | solution.py:12
  93.1 3.0 fusion.8
  96.1 0.6 fusion.11
  96.8 0.6 convolution_subtract_fusion
  97.3 0.6 fusion.20
  98.0 1.0 pad_maximum_fusion.2
  99.3 1.3 slice.86
  100.6 0.5 concatenate.13
  101.1 1.2 copy.59
  102.2 47.1 %all-gather.10.cloned.1.call-done = f32[2048,1024]{1,0:T(8,128)} async-done(((f32[256,1024]{1,0:T(8,128)}), f32[2048,1024]{1,0:T(8,128)}) %all-gather.10.cloned.1.call-update) | async-done | bytes 8388624 | tf_op jit(solution)/shard_map/all_gather | solution.py:12
  149.4 1.3 slice.92
  151.4 2.7 pad_maximum_fusion
  154.2 20.9 %copy.63 = f32[8,1,256,4,1,256]{2,5,3,0,4,1:T(8,128)} copy(f32[8,1,256,4,1,256]{5,4,3,2,1,0:T(1,128)} %param.4) | data formatting | bytes 16777216 | tf_op args[0]
  175.4 17.2 %convolution_bitcast_fusion.1 = f32[8,256,1024]{1,2,0:T(8,128)} fusion(f32[2,8,1,256,256]{4,3,1,2,0:T(8,128)} %bitcast.124, f32[2048,1024]{1,0:T(8,128)} %all-gather.8.cloned.1.call-done), kind=kOutput, calls=%fused_computation.11 | convolution fusion | flops 6442450944 | bytes 11534336 | tf_op jit(solution)/shard_map/rab,bc->rac/dot_general | solution.py:35
  192.6 1.3 copy.69
  193.9 16.5 %convolution_bitcast_fusion = f32[8,256,1024]{1,2,0:T(8,128)S(1)} fusion(f32[2,8,1,256,256]{4,3,1,2,0:T(8,128)} %bitcast.125, f32[2048,1024]{1,0:T(8,128)} %all-gather.10.cloned.1.call-done), kind=kOutput, calls=%fused_computation.10 | convolution fusion | flops 6442450944 | bytes 11534336 | tf_op jit(solution)/shard_map/rab,bc->rac/dot_general | solution.py:35
  210.5 2.8 fusion
  213.3 2.1 fusion.29
  215.4 2.2 copy.85
  217.6 2.1 copy.86
  219.7 2.0 copy.87
  221.7 2.1 copy.88
  223.8 2.0 copy.89
  225.8 2.0 copy.90
  227.9 1.0 copy.91
  228.9 1.0 copy.92
  229.9 2.0 bitcast_dynamic-update-slice_fusion.9
  231.9 1.9 bitcast_dynamic-update-slice_fusion.8
  233.8 1.9 bitcast_dynamic-update-slice_fusion.7
  235.6 1.9 bitcast_dynamic-update-slice_fusion.6
  237.5 0.8 bitcast_dynamic-update-slice_fusion.5
  238.3 0.8 bitcast_dynamic-update-slice_fusion.4
  239.2 0.8 bitcast_dynamic-update-slice_fusion.3
  240.0 0.8 bitcast_dynamic-update-slice_fusion.2
  240.8 4.8 %all-to-all-start = ((f32[8,4,1,256,1,1,128]{6,3,1,5,4,2,0:T(8,128)}), f32[8,4,1,256,1,1,128]{6,3,1,5,4,2,0:T(8,128)}, u32[]{:S(2)}, u32[]{:S(2)}) async-start(f32[8,4,1,256,1,1,128]{6,3,1,5,4,2,0:T(8,128)} %bitcast_dynamic-update-slice_fusion.2), calls=%async_computation | async-start | bytes 8388608 | tf_op jit(solution)/shard_map/all_to_all | solution.py:77
  245.6 48.9 %all-to-all-done = f32[8,4,1,256,1,1,128]{6,3,1,5,4,2,0:T(8,128)} async-done(((f32[8,4,1,256,1,1,128]{6,3,1,5,4,2,0:T(8,128)}), f32[8,4,1,256,1,1,128]{6,3,1,5,4,2,0:T(8,128)}, u32[]{:S(2)}, u32[]{:S(2)}) %all-to-all-start) | async-done | bytes 4194336 | tf_op jit(solution)/shard_map/all_to_all | solution.py:77
  294.5 11.4 %copy.79 = f32[4,8,256,1,1,128]{5,4,3,2,1,0:T(1,128)} copy(f32[4,8,256,1,1,128]{5,2,0,1,4,3:T(8,128)} %bitcast.33) | data formatting | bytes 8388608
  305.9 44.9 %all-gather.6.cloned.1.call-done = f32[512,4,16,256]{3,0,1,2:T(8,128)} async-done(((f32[512,4,1,256]{3,0,1,2:T(8,128)}), f32[512,4,16,256]{3,0,1,2:T(8,128)}) %all-gather.6.cloned.1.call-update) | async-done | bytes 33554448 | tf_op jit(solution)/shard_map/all_gather | solution.py:64
  350.8 28.3 %copy.95 = f32[512,4,16,256]{3,2,1,0:T(8,128)S(1)} copy(f32[512,4,16,256]{3,0,1,2:T(8,128)} %all-gather.6.cloned.1.call-done) | data formatting | bytes 67108864 | tf_op jit(solution)/shard_map/all_gather | solution.py:64
  379.1 6.6 %constant_dynamic-slice_fusion.2 = f32[512,4,2,1,256]{4,3,2,1,0:T(1,128)} fusion(f32[512,4,2,8,256]{4,3,2,1,0:T(8,128)S(1)} %bitcast.120, s32[]{:T(128)S(6)} %select_n.57), kind=kLoop, calls=%fused_computation.67 | loop fusion | bytes 8388612 | tf_op jit(solution)/shard_map/jit(dynamic_index_in_dim)/dynamic_slice | solution.py:68
  385.7 10.9 %copy.62 = f32[512,4,2,1,256]{0,4,2,1,3:T(8,128)} copy(f32[512,4,2,1,256]{4,3,2,1,0:T(1,128)} %constant_dynamic-slice_fusion.2) | data formatting | bytes 8388608 | tf_op jit(solution)/shard_map/jit(dynamic_index_in_dim)/dynamic_slice | solution.py:68
  396.7 17.5 %convolution_multiply_fusion = f32[2048,1024]{1,0:T(8,128)} fusion(f32[512,2048]{0,1:T(8,128)} %bitcast.121, f32[256,1024]{1,0:T(8,128)S(1)} %slice.92, f32[256,1024]{1,0:T(8,128)S(1)} %slice.86), kind=kOutput, calls=%fused_computation.5 | convolution fusion | flops 12887523328 | bytes 14680064 | tf_op jit(solution)/shard_map/dot_general | solution.py:70
  414.2 13.5 %reshape.110 = f32[8,1,256,4,1,256]{5,4,3,2,1,0:T(1,128)} reshape(f32[2048,1024]{1,0:T(8,128)} %convolution_multiply_fusion) | data formatting | bytes 16777216 | tf_op jit(solution)/shard_map/reshape | solution.py:73
  (32 shorter events, 1.7 us)
Async XLA Ops:
  7.2 86.0 %all-gather.8.cloned.1.call-start = ((), (), s32[]{:S(2)}) async-start(), calls=%async_computation.2 | async-start | bytes 9437184 | tf_op jit(solution)/shard_map/all_gather | solution.py:12
  39.4 110.0 %all-gather.10.cloned.1.call-start = ((), (), s32[]{:S(2)}) async-start(), calls=%async_computation.3 | async-start | bytes 9437184 | tf_op jit(solution)/shard_map/all_gather | solution.py:12
  99.0 251.8 %all-gather.6.cloned.1.call-start = ((), (), s32[]{:S(2)}) async-start(), calls=%async_computation.1 | async-start | bytes 35651584 | tf_op jit(solution)/shard_map/all_gather | solution.py:64
  193.9 16.6 %copy-start = (f32[8,256,1024]{1,2,0:T(8,128)S(1)}, f32[8,256,1024]{1,2,0:T(8,128)}, u32[]{:S(2)}) copy-start(f32[8,256,1024]{1,2,0:T(8,128)} %convolution_bitcast_fusion.1) | copy-start | bytes 25165828
  193.9 16.6 %copy-start.1 = (f32[256,1024]{0,1:T(8,128)S(1)}, f32[256,1024]{0,1:T(8,128)}, u32[]{:S(2)}) copy-start(f32[256,1024]{0,1:T(8,128)} %copy.69) | copy-start | bytes 3145732
  228.9 10.3 %copy-start.2 = (f32[4,1,256,1,1,128]{5,2,0,4,3,1:T(8,128)S(1)}, f32[4,1,256,1,1,128]{5,2,0,4,3,1:T(8,128)}, u32[]{:S(2)}) copy-start(f32[4,1,256,1,1,128]{5,2,0,4,3,1:T(8,128)} %copy.91) | copy-start | bytes 1572868
  229.9 7.6 %copy-start.5 = (f32[4,1,256,1,1,128]{5,2,0,4,3,1:T(8,128)S(1)}, f32[4,1,256,1,1,128]{5,2,0,4,3,1:T(8,128)}, u32[]{:S(2)}) copy-start(f32[4,1,256,1,1,128]{5,2,0,4,3,1:T(8,128)} %copy.89) | copy-start | bytes 1572868
  229.9 8.5 %copy-start.4 = (f32[4,1,256,1,1,128]{5,2,0,4,3,1:T(8,128)S(1)}, f32[4,1,256,1,1,128]{5,2,0,4,3,1:T(8,128)}, u32[]{:S(2)}) copy-start(f32[4,1,256,1,1,128]{5,2,0,4,3,1:T(8,128)} %copy.90) | copy-start | bytes 1572868
  229.9 10.1 %copy-start.3 = (f32[4,1,256,1,1,128]{5,2,0,4,3,1:T(8,128)S(1)}, f32[4,1,256,1,1,128]{5,2,0,4,3,1:T(8,128)}, u32[]{:S(2)}) copy-start(f32[4,1,256,1,1,128]{5,2,0,4,3,1:T(8,128)} %copy.92) | copy-start | bytes 1572868
  240.8 53.7 %all-to-all-start = ((f32[8,4,1,256,1,1,128]{6,3,1,5,4,2,0:T(8,128)}), f32[8,4,1,256,1,1,128]{6,3,1,5,4,2,0:T(8,128)}, u32[]{:S(2)}, u32[]{:S(2)}) async-start(f32[8,4,1,256,1,1,128]{6,3,1,5,4,2,0:T(8,128)} %bitcast_dynamic-update-slice_fusion.2), calls=%async_computation | async-start | bytes 8388608 | tf_op jit(solution)/shard_map/all_to_all | solution.py:77
Sparse Core Ops, SparseCore 0:
  39.5 53.6 all-gather.7
  99.2 50.1 all-gather.9
  154.3 196.5 all-gather.5
